TPU v7x, 256 devices: a whole 4x4x8 slice. The times are simulated.
256 devices in a mesh: group: 8 (over z), rank: 32 (over y, x, core).
Axes of the slice: x: 4, y: 4, z: 8, core: 2. Of those that a mesh axis runs over, the one named last changes fastest.
Arguments:
- queries: bfloat16 [4096, 64, 576], P(('group', 'rank')), parts along dimension 0, may hold values from -20 to 20
- cache_pool: bfloat16 [4096, 32, 576], P(('group', 'rank')), parts along dimension 0, may hold values from -6 to 6
- lengths: int32 [4096], P(('group', 'rank')), parts along dimension 0, may hold values from 0 to 128, as said below
- block_table: int32 [4096, 4], P(('group', 'rank')), parts along dimension 0, may hold values from 0 to 15, as said below
- residual: bfloat16 [4096, 7168], P(('group', 'rank')), parts along dimension 0, may hold values from -3 to 3
- norm_gain: bfloat16 [7168], replicated, may hold values from 0.099609375 to 1.8984375
- uv_weight: bfloat16 [64, 512, 128], P('rank'), may hold values from -0.25 to 0.25
- out_weight: bfloat16 [8192, 7168], P(None, 'rank'), may hold values from -0.0625 to 0.0625
- gate_weight: bfloat16 [7168, 9216], P(None, 'rank'), may hold values from -0.0625 to 0.0625
- up_weight: bfloat16 [7168, 9216], P(None, 'rank'), may hold values from -0.0625 to 0.0625
Outputs:
- mixed: bfloat16 [4096, 7168], P(('group', 'rank')), parts along dimension 0
- activ: bfloat16 [4096, 9216], P('group', 'rank'), parts along dimension 0
There are 8 independent parts, one for each index of `group`. A program takes and returns all parts, laid end to end along the dimension named above; an argument that names none is the same for every part. Nothing has to cross between parts.
Inputs may be any that keep to these rules, and one draw needn't show every extreme that they name: `lengths`: the live slots of each rank are its first ones, at least one a rank; some rank has all 16 slots live and some rank exactly one. A live slot holds 1 to 128 tokens and the longest reaches that in every draw. `block_table`: A slot's first ceil(lengths / 32) entries name distinct pages of its own rank, no page shared between slots; the other entries are 0.
All inputs are finite; a program needn't handle non-finite values.
Results may differ from a plain program's by a relative error of at most 0.0075.
Values may be sent and summed in bfloat16 or wider, within the bound.
A program may use at most 64 MiB of HBM per device.

v0:
```python
import jax
import jax.numpy as jnp
from jax import lax
from jax.sharding import PartitionSpec as P

ROPE = 64


score_scale = 192.0 ** (-0.5)


def attend(queries, cache_pool, lengths, block_table):
    slots, heads, width = queries.shape
    latent = width - ROPE
    keys_all = cache_pool[block_table].reshape(slots, -1, width)
    scores = (
        jnp.einsum("rhc,rtc->rht", queries, keys_all, preferred_element_type=jnp.float32)
        * score_scale
    )
    position = jnp.arange(keys_all.shape[1], dtype=jnp.int32)
    valid = position[None, None, :] < lengths[:, None, None]
    scores = jnp.where(valid, scores, -1e30)
    peak = jnp.max(scores, axis=2, keepdims=True)
    expo = jnp.where(valid, jnp.exp(scores - peak), 0.0)
    total = jnp.sum(expo, axis=2, keepdims=True)
    total = jnp.where(total > 0.0, total, 1.0)
    weights = (expo / total).astype(jnp.bfloat16)
    context = jnp.einsum(
        "rht,rtc->rhc", weights, keys_all[:, :, :latent], preferred_element_type=jnp.float32
    )
    return context.astype(jnp.bfloat16)


def norm_rows(mixed, norm_gain):
    values = mixed.astype(jnp.float32)
    factor = lax.rsqrt(jnp.mean(values * values, axis=-1, keepdims=True) + 1e-06)
    return (values * factor * norm_gain.astype(jnp.float32)).astype(jnp.bfloat16)


def gated_units(normed, gate_weight, up_weight):
    gate = jnp.dot(normed, gate_weight, preferred_element_type=jnp.float32)
    upper = jnp.dot(normed, up_weight, preferred_element_type=jnp.float32)
    return (jax.nn.silu(gate) * upper).astype(jnp.bfloat16)


def per_device(
    queries,
    cache_pool,
    lengths,
    block_table,
    residual,
    norm_gain,
    uv_weight,
    out_weight,
    gate_weight,
    up_weight,
):
    context = attend(queries, cache_pool, lengths, block_table)
    arrived = lax.all_to_all(context, "rank", split_axis=1, concat_axis=0, tiled=True)
    values = jnp.einsum(
        "bhl,hld->bhd", arrived, uv_weight, preferred_element_type=jnp.float32
    ).astype(jnp.bfloat16)
    flattened = values.reshape(values.shape[0], -1)
    attended = jnp.dot(
        lax.all_gather(flattened, "rank", axis=1, tiled=True),
        out_weight,
        preferred_element_type=jnp.float32,
    )
    residual_cols = lax.all_to_all(residual, "rank", split_axis=1, concat_axis=0, tiled=True)
    mixed_cols = (residual_cols.astype(jnp.float32) + attended).astype(jnp.bfloat16)
    mixed = lax.all_to_all(mixed_cols, "rank", split_axis=0, concat_axis=1, tiled=True)
    normed = norm_rows(mixed, norm_gain)
    activ = gated_units(lax.all_gather(normed, "rank", axis=0, tiled=True), gate_weight, up_weight)
    return (mixed, activ)


def solution(mesh):
    placed = (
        P(("group", "rank"), None, None),
        P(("group", "rank"), None, None),
        P(("group", "rank")),
        P(("group", "rank"), None),
        P(("group", "rank"), None),
        P(),
        P("rank", None, None),
        P(None, "rank"),
        P(None, "rank"),
        P(None, "rank"),
    )
    return jax.shard_map(
        per_device,
        mesh=mesh,
        in_specs=placed,
        out_specs=(P(("group", "rank"), None), P("group", "rank")),
        check_vma=False,
    )
```

profile of v0, /device:TPU:1, one launch (start us, length us, event | category | flops | bytes accessed | tf_op | source)
XLA Modules:
  0.0 198.8 jit_solution(6307767126683852981)
XLA Ops:
  7.2 0.0 copy-start
  7.2 0.0 all-gather.3.cloned.1.call-start
  7.2 0.8 compare_select_fusion.1
  8.0 0.1 copy.34
  8.1 0.1 reshape.60
  8.2 0.7 iota_compare_fusion
  8.9 3.4 %gather_fusion = bf16[64,32,576]{2,1,0:T(8,128)(2,1)} fusion(bf16[16,32,576]{2,1,0:T(8,128)(2,1)} %param.11, s32[1024]{0:T(1024)S(1)} %pad_clamp_fusion), kind=kCustom, calls=%fused_computation | custom fusion | bytes 4718848 | tf_op jit(solution)/shard_map/gather | solution.py:15
  12.4 0.0 copy-done
  12.4 2.9 %fusion.10 = f32[16,64,128]{2,1,0:T(8,128)S(1)} fusion(bf16[16,128,576]{2,1,0:T(8,128)(2,1)} %bitcast.28, bf16[16,64,576]{2,1,0:T(8,128)(2,1)S(1)} %copy-done, pred[16,128]{1,0:T(8,128)(4,1)S(1)} %iota_compare_fusion), kind=kOutput, calls=%fused_computation.11 | convolution fusion | flops 151257088 | bytes 4065280 | tf_op jit(solution)/shard_map/rhc,rtc->rht/dot_general | solution.py:17
  15.3 0.3 fusion.16
  15.6 3.5 %fusion.3 = bf16[16,64,512]{2,1,0:T(8,128)(2,1)S(1)} fusion(bf16[16,128,576]{2,1,0:T(8,128)(2,1)} %bitcast.29, f32[16,64]{1,0:T(8,128)S(1)} %compare_select_fusion, f32[16,64,128]{2,1,0:T(8,128)S(1)} %fusion.10, pred[16,128]{1,0:T(8,128)(4,1)S(1)} %iota_compare_fusion), kind=kOutput, calls=%fused_computation.4 | convolution fusion | flops 135267456 | bytes 4204544 | tf_op jit(solution)/shard_map/rht,rtc->rhc/dot_general | solution.py:28
  19.1 0.0 copy-start.2
  19.1 0.0 copy-start.3
  19.2 0.6 copy.36
  19.8 25.6 %all_to_all.50 = bf16[16,64,512]{2,0,1:T(8,128)(2,1)S(1)} all-to-all(bf16[16,64,512]{2,0,1:T(8,128)(2,1)S(1)} %copy.36), channel_id=1, replica_groups=mesh['group'=8,'rank'=32] {'rank'}, dimensions={1} | all-to-all | bytes 2097152 | tf_op jit(solution)/shard_map/all_to_all | solution.py:59
  45.3 0.1 copy.37
  45.4 0.0 copy-done.2
  45.4 1.2 convolution_convert_fusion
  46.6 0.0 all-gather.3.cloned.1.call-update
  46.6 0.0 copy-done.3
  46.6 0.4 all_to_all.37
  47.0 0.2 copy.33
  47.2 12.4 %all_to_all.51 = bf16[16,32,224]{2,0,1:T(8,128)(2,1)S(1)} all-to-all(bf16[16,32,224]{2,0,1:T(8,128)(2,1)S(1)} %copy.33), channel_id=1, replica_groups=mesh['group'=8,'rank'=32] {'rank'}, dimensions={1} | all-to-all | bytes 458752 | tf_op jit(solution)/shard_map/all_to_all | solution.py:69
  59.6 0.2 copy.39
  59.8 0.0 copy-start.4
  59.9 44.2 %all-gather.3.cloned.1.call-done = bf16[512,8192]{0,1:T(8,128)(2,1)} async-done(((bf16[512,256]{0,1:T(8,128)(2,1)}), bf16[512,8192]{0,1:T(8,128)(2,1)}) %all-gather.3.cloned.1.call-update) | async-done | bytes 8388624 | tf_op jit(solution)/shard_map/all_gather | solution.py:65
  104.1 6.6 %fusion.12 = bf16[512,224]{0,1:T(8,128)(2,1)S(1)} fusion(f32[512,224]{0,1:T(8,128)S(1)} %copy.39, bf16[8192,224]{0,1:T(8,128)(2,1)} %param.17, bf16[512,8192]{0,1:T(8,128)(2,1)} %all-gather.3.cloned.1.call-done), kind=kOutput, calls=%fused_computation.15 | convolution fusion | flops 1879277568 | bytes 12746752 | tf_op jit(solution)/shard_map/dot_general | solution.py:64
  110.6 0.8 copy.40
  111.5 5.5 %all-to-all-start.2 = ((bf16[32,16,224]{2,1,0:T(8,128)(2,1)}), bf16[32,16,224]{2,1,0:T(8,128)(2,1)S(1)}, u32[]{:S(2)}, u32[]{:S(2)}) async-start(bf16[32,16,224]{2,1,0:T(8,128)(2,1)} %bitcast.9), calls=%async_computation.2 | async-start | bytes 524288 | tf_op jit(solution)/shard_map/all_to_all | solution.py:71
  117.0 0.2 all-gather.5.cloned.1.call-start
  117.2 0.0 copy-done.4
  117.2 8.6 %all-to-all-done.2 = bf16[32,16,224]{2,1,0:T(8,128)(2,1)S(1)} async-done(((bf16[32,16,224]{2,1,0:T(8,128)(2,1)}), bf16[32,16,224]{2,1,0:T(8,128)(2,1)S(1)}, u32[]{:S(2)}, u32[]{:S(2)}) %all-to-all-start.2) | async-done | bytes 229408 | tf_op jit(solution)/shard_map/all_to_all | solution.py:71
  125.9 0.1 copy.41
  126.0 0.4 all_to_all.46
  126.3 0.0 copy-start.1
  126.3 0.2 multiply_reduce_fusion
  126.5 0.8 multiply_convert_fusion
  127.4 0.0 all-gather.5.cloned.1.call-update
  127.4 54.0 %all-gather.5.cloned.1.call-done = bf16[512,7168]{1,0:T(8,128)(2,1)} async-done(((bf16[16,7168]{1,0:T(8,128)(2,1)}), bf16[512,7168]{1,0:T(8,128)(2,1)}) %all-gather.5.cloned.1.call-update) | async-done | bytes 7340048 | tf_op jit(solution)/shard_map/all_gather | solution.py:73
  181.4 0.0 copy-start.5
  181.4 0.0 copy-start.6
  181.4 6.7 %fusion.17 = f32[512,288]{0,1:T(8,128)S(1)} fusion(bf16[512,7168]{1,0:T(8,128)(2,1)} %all-gather.5.cloned.1.call-done, bf16[7168,288]{0,1:T(8,128)(2,1)} %param.18), kind=kOutput, calls=%fused_computation.28 | convolution fusion | flops 2113929216 | bytes 12058624 | tf_op jit(solution)/shard_map/dot_general | solution.py:41
  188.1 0.0 copy-done.1
  188.1 0.0 copy-done.5
  188.1 0.8 copy-done.6
  188.9 3.1 %fusion.11 = bf16[512,288]{0,1:T(8,128)(2,1)} fusion(bf16[512,7168]{1,0:T(8,128)(2,1)S(1)} %copy-done.5, bf16[7168,288]{0,1:T(8,128)(2,1)S(1)} %copy-done.6, f32[512,288]{0,1:T(8,128)S(1)} %fusion.17), kind=kOutput, calls=%fused_computation.12 | convolution fusion | flops 2114813952 | bytes 12353536 | tf_op jit(solution)/shard_map/dot_general | solution.py:42
  (5 shorter events, 0.1 us)
Async XLA Ops:
  7.2 5.2 %copy-start = (bf16[16,64,576]{2,1,0:T(8,128)(2,1)S(1)}, bf16[16,64,576]{2,1,0:T(8,128)(2,1)}, u32[]{:S(2)}) copy-start(bf16[16,64,576]{2,1,0:T(8,128)(2,1)} %param.10) | copy-start | bytes 3538948
  7.2 96.9 %all-gather.3.cloned.1.call-start = ((), (), s32[]{:S(2)}) async-start(), calls=%async_computation.3 | async-start | bytes 8650752 | tf_op jit(solution)/shard_map/all_gather | solution.py:65
  19.1 26.3 %copy-start.2 = (bf16[2,512,128]{2,1,0:T(8,128)(2,1)S(1)}, bf16[2,512,128]{2,1,0:T(8,128)(2,1)}, u32[]{:S(2)}) copy-start(bf16[2,512,128]{2,1,0:T(8,128)(2,1)} %param.16) | copy-start | bytes 786436
  19.1 27.5 %copy-start.3 = (bf16[16,7168]{1,0:T(8,128)(2,1)S(1)}, bf16[16,7168]{1,0:T(8,128)(2,1)}, u32[]{:S(2)}) copy-start(bf16[16,7168]{1,0:T(8,128)(2,1)} %param.14) | copy-start | bytes 688132
  59.8 57.4 %copy-start.4 = (bf16[7168]{0:T(1024)(128)(2,1)S(1)}, bf16[7168]{0:T(1024)(128)(2,1)}, u32[]{:S(2)}) copy-start(bf16[7168]{0:T(1024)(128)(2,1)} %param.15) | copy-start | bytes 43012
  111.5 14.4 %all-to-all-start.2 = ((bf16[32,16,224]{2,1,0:T(8,128)(2,1)}), bf16[32,16,224]{2,1,0:T(8,128)(2,1)S(1)}, u32[]{:S(2)}, u32[]{:S(2)}) async-start(bf16[32,16,224]{2,1,0:T(8,128)(2,1)} %bitcast.9), calls=%async_computation.2 | async-start | bytes 524288 | tf_op jit(solution)/shard_map/all_to_all | solution.py:71
  117.0 64.4 %all-gather.5.cloned.1.call-start = ((), (), s32[]{:S(2)}) async-start(), calls=%async_computation.4 | async-start | bytes 7569408 | tf_op jit(solution)/shard_map/all_gather | solution.py:73
  126.3 61.8 %copy-start.1 = (bf16[16,7168]{1,0:T(8,128)(2,1)}, bf16[16,7168]{1,0:T(8,128)(2,1)S(1)}, u32[]{:S(2)}) copy-start(bf16[16,7168]{1,0:T(8,128)(2,1)S(1)} %all_to_all.46) | copy-start | bytes 688132
  181.4 6.8 %copy-start.5 = (bf16[512,7168]{1,0:T(8,128)(2,1)S(1)}, bf16[512,7168]{1,0:T(8,128)(2,1)}, u32[]{:S(2)}) copy-start(bf16[512,7168]{1,0:T(8,128)(2,1)} %all-gather.5.cloned.1.call-done) | copy-start | bytes 22020100
  181.4 7.5 %copy-start.6 = (bf16[7168,288]{0,1:T(8,128)(2,1)S(1)}, bf16[7168,288]{0,1:T(8,128)(2,1)}, u32[]{:S(2)}) copy-start(bf16[7168,288]{0,1:T(8,128)(2,1)} %param.19) | copy-start | bytes 12386308
Sparse Core Ops, SparseCore 0:
  46.7 57.2 all-gather.2
  127.5 53.8 all-gather.4
where the time goes:
time: 199 us
  waiting for transfers between devices  107 us (54%)
  blocking collectives  38 us (19%)
  matrix products  23.9 us (12%)
  between operations  14.2 us (7%)
  local copies, waits for them, and re-layouts  7.06 us (4%)
  starting transfers between devices  5.73 us (3%)
  other arithmetic  2.95 us (1%)
    all_gather x1, waiting for transfers between devices, per_device(): lax.all_gather(normed, 'rank', axis=0, tiled=True)  54 us
    all_gather x1, waiting for transfers between devices, per_device(): lax.all_gather(flattened, 'rank', axis=1, tiled=True)  44.2 us
    all_to_all x1, blocking collectives, per_device(): lax.all_to_all(context, 'rank', split_axis=1, concat_axis=0, tiled=True)  25.6 us
    all_to_all x1, blocking collectives, per_device(): lax.all_to_all(residual, 'rank', split_axis=1, concat_axis=0, tiled=True)  12.4 us
    all_to_all x1, waiting for transfers between devices, per_device(): lax.all_to_all(mixed_cols, 'rank', split_axis=0, concat_axis=1, tiled=True)  8.65 us
    dot_general x1, matrix products, gated_units(): gate = jnp.dot(normed, gate_weight, preferred_element_type=jnp.float32)  6.73 us
    dot_general x1, matrix products, per_device(): jnp.dot(lax.all_gather(flattened, 'rank', axis=1, tiled=True), out_weight...  6.55 us
    all_to_all x1, starting transfers between devices, per_device(): lax.all_to_all(mixed_cols, 'rank', split_axis=0, concat_axis=1, tiled=True)  5.47 us
  transfers between devices with their start and end apart: 3, of which 3 were waited for; matrix products, arithmetic and copies ran while one was open for 0% of the time, Pallas kernels for 0%

commit v1 on v0

v1 whole, which is shorter than its diff:
```python
import jax
import jax.numpy as jnp
from jax import lax
from jax.experimental import pallas as pl
from jax.experimental.pallas import tpu as pltpu
from jax.sharding import PartitionSpec as P

F32 = jnp.float32
BF16 = jnp.bfloat16
MESH = pl.DeviceIdType.MESH

N = 32
SLOTS = 16
HEADS = 64
LAT = 512
WIDTH = 576
TOK = 512
PAGE = 32
MAXP = 4
D = 7168
COLS = 224
HID = 288
LANES = 256

NC = 2
SL = SLOTS // NC
RC = N * SL
HALF = RC // 2
SKEW = 8
STEPS = 33

score_scale = 192.0 ** (-0.5)


def kernel(
    len_ref, bt_ref, q_hbm, pool_hbm, res_hbm, gain_ref, uv_hbm, ow_hbm, gw_hbm, uw_hbm,
    mixed_ref, activ_ref,
    q_v, pool_v, res_v, uv_v, ow_v, gw_v, uw_v,
    mask_v, ctx, sbuf, cbuf, rs, rr, vbuf, mbuf, acc, accg, accu, ssq,
    load_sem, own_sem, res_send, res_recv, a2a_send, a2a_recv, ag_send, a_recv, b_recv, s_recv,
):
    me = lax.axis_index("rank")
    core = me % 2
    xx = (me // 2) % 4
    yy = me // 8
    sa = (1 - core) * 2 + core * 8
    sb = (1 - core) * 8 + core * 2
    a = (1 - core) * xx + core * yy
    b = (1 - core) * yy + core * xx
    sibling = me + 1 - 2 * core

    def rank_at(pa, pb):
        return pa * sa + pb * sb + core

    up_a, down_a = rank_at((a + 1) % 4, b), rank_at((a + 3) % 4, b)
    up_b, down_b = rank_at(a, (b + 1) % 4), rank_at(a, (b + 3) % 4)

    loads = [
        pltpu.make_async_copy(src, dst, load_sem.at[i])
        for i, (src, dst) in enumerate(
            [
                (q_hbm, q_v),
                (pool_hbm, pool_v),
                (res_hbm, res_v),
                (uv_hbm, uv_v),
                (ow_hbm, ow_v),
                (gw_hbm, gw_v.at[pl.ds(0, D)]),
                (uw_hbm, uw_v.at[pl.ds(0, D)]),
            ]
        )
    ]
    for load in loads:
        load.start()

    barrier = pltpu.get_barrier_semaphore()

    def greet(k, carry):
        pl.semaphore_signal(barrier, inc=1, device_id={"rank": (me + k) % N}, device_id_type=MESH)
        return carry

    lax.fori_loop(1, N, greet, 0)

    lane = lax.broadcasted_iota(jnp.int32, (1, TOK), 1)
    page_of = lane // PAGE
    offset = lane % PAGE
    for slot in range(SLOTS):
        n = len_ref[slot]
        valid = jnp.zeros((1, TOK), F32)
        for m in range(MAXP):
            hit = (page_of == bt_ref[slot, m]) & (offset + m * PAGE < n)
            valid = jnp.where(hit, 1.0, valid)
        mask_v[slot // 4, slot % 4 : slot % 4 + 1, :] = valid
    gw_v[D:, :] = jnp.zeros((32, HID), BF16)
    uw_v[D:, :] = jnp.zeros((32, HID), BF16)
    acc[...] = jnp.zeros_like(acc)
    accg[...] = jnp.zeros_like(accg)
    accu[...] = jnp.zeros_like(accu)
    ssq[...] = jnp.zeros_like(ssq)

    loads[2].wait()
    for r in range(N):
        rs[r, :, 0:COLS] = res_v[:, r * COLS : (r + 1) * COLS]
        rs[r, :, COLS:LANES] = jnp.zeros((SLOTS, LANES - COLS), BF16)
    loads[0].wait()
    loads[1].wait()

    pl.semaphore_wait(barrier, N - 1)

    def dest_of(k):
        p = (k * 11) % N
        return ((yy + p // 8) % 4) * 8 + ((xx + (p // 2) % 4) % 4) * 2 + (core + p % 2) % 2

    def send_res(k, carry):
        to = dest_of(k)
        pltpu.make_async_remote_copy(
            src_ref=rs.at[to], dst_ref=rr.at[me], send_sem=res_send, recv_sem=res_recv,
            device_id={"rank": to}, device_id_type=MESH,
        ).start()
        return carry

    lax.fori_loop(1, N, send_res, 0)
    own_res = pltpu.make_async_copy(rs.at[me], rr.at[me], own_sem.at[NC])
    own_res.start()

    def attend(first, carry):
        q = q_v[pl.ds(first * 4, 4)].reshape(4 * HEADS, WIDTH)
        scores = lax.dot_general(
            q, pool_v[...].reshape(TOK, WIDTH), (((1,), (1,)), ((), ())), preferred_element_type=F32
        ) * score_scale
        ok = jnp.broadcast_to(
            mask_v[first][:, None, :], (4, HEADS, TOK)
        ).reshape(4 * HEADS, TOK) > 0.0
        scores = jnp.where(ok, scores, -1e30)
        peak = jnp.max(scores, axis=1, keepdims=True)
        expo = jnp.where(ok, jnp.exp(scores - peak), 0.0)
        total = jnp.sum(expo, axis=1, keepdims=True)
        total = jnp.where(total > 0.0, total, 1.0)
        weights = (expo / total).astype(BF16)
        out = jnp.dot(weights, pool_v[...].reshape(TOK, WIDTH)[:, :LAT], preferred_element_type=F32)
        for part in range(LAT // 128):
            ctx[part, pl.ds(pl.multiple_of(first * 4 * HEADS, 4 * HEADS), 4 * HEADS), :] = out[
                :, part * 128 : (part + 1) * 128
            ]
        return carry

    own_ctx = []
    for ch in range(NC):
        lax.fori_loop(ch * SL // 4, (ch + 1) * SL // 4, attend, 0)

        def pack(r, carry, ch=ch):
            for part in range(LAT // 128):
                pair = [
                    ctx[part, pl.ds(ch * SL * HEADS + 2 * r + h, SL, stride=HEADS), :] for h in range(2)
                ]
                sbuf[ch, r, :, part * 128 : (part + 1) * 128] = jnp.concatenate(pair, axis=0).astype(BF16)
            return carry

        lax.fori_loop(0, N, pack, 0)

        def send_ctx(k, carry, ch=ch):
            to = dest_of(k)
            pltpu.make_async_remote_copy(
                src_ref=sbuf.at[ch, to], dst_ref=cbuf.at[ch, me],
                send_sem=a2a_send.at[ch], recv_sem=a2a_recv.at[ch],
                device_id={"rank": to}, device_id_type=MESH,
            ).start()
            return carry

        lax.fori_loop(1, N, send_ctx, 0)
        own_ctx.append(pltpu.make_async_copy(sbuf.at[ch, me], cbuf.at[ch, me], own_sem.at[ch]))
        own_ctx[ch].start()

    for load in loads[3:]:
        load.wait()
    own_res.wait()
    pltpu.make_async_remote_copy(
        src_ref=rs.at[pl.ds(0, N - 1)], dst_ref=rr.at[pl.ds(0, N - 1)], send_sem=res_send, recv_sem=res_recv,
        device_id={"rank": sibling}, device_id_type=MESH,
    ).wait()

    def turn(j):
        return (4 - j + (j // 2) * 3 + (j // 3) * 2) % 4

    def place(k):
        middle = (k // 4 + 1) // 2 - 2 * (k // 12)
        last = k // 12
        j = (1 - middle) * (k % 4) + middle * (((k + 12) % 16) // 2)
        i = middle * (1 + k % 2) + last * 3
        return j, i

    def shard(k):
        j, i = place(k)
        return rank_at((a + turn(j)) % 4, (b + turn(i)) % 4)

    def other_shard(k):
        j, i = place(k)
        return ((b + turn(j)) % 4) * sb + ((a + turn(i)) % 4) * sa + (1 - core)

    def action(g, ch, k, buf):
        s = shard(k)
        j, i = place(k)
        full = buf.at[ch, s]
        top = buf.at[ch, s, pl.ds(0, HALF)]
        bottom = buf.at[ch, s, pl.ds(HALF, HALF)]

        def push(ref, sem, to):
            pltpu.make_async_remote_copy(
                src_ref=ref, dst_ref=ref, send_sem=ag_send.at[g, ch], recv_sem=sem,
                device_id={"rank": to}, device_id_type=MESH,
            ).start()

        def arrive(ref, sem):
            pltpu.make_async_remote_copy(
                src_ref=ref, dst_ref=ref, send_sem=ag_send.at[g, ch], recv_sem=sem,
                device_id={"rank": sibling}, device_id_type=MESH,
            ).wait_recv()

        @pl.when(k == 0)
        def _():
            push(full, a_recv.at[g, ch, 0], up_a)
            push(full, a_recv.at[g, ch, 1], down_a)

        @pl.when(k == 1)
        def _():
            arrive(full, a_recv.at[g, ch, 0])
            push(top, a_recv.at[g, ch, 2], up_a)

        @pl.when(k == 2)
        def _():
            arrive(full, a_recv.at[g, ch, 1])
            push(bottom, a_recv.at[g, ch, 3], down_a)

        @pl.when(k == 3)
        def _():
            arrive(top, a_recv.at[g, ch, 2])
            arrive(bottom, a_recv.at[g, ch, 3])

        @pl.when(k < 4)
        def _():
            push(full, b_recv.at[g, ch, j * 4], up_b)
            push(full, b_recv.at[g, ch, j * 4 + 1], down_b)

        @pl.when((k >= 4) & (k < 12) & (k % 2 == 0))
        def _():
            arrive(full, b_recv.at[g, ch, j * 4])
            push(top, b_recv.at[g, ch, j * 4 + 2], up_b)

        @pl.when((k >= 4) & (k < 12) & (k % 2 == 1))
        def _():
            arrive(full, b_recv.at[g, ch, j * 4 + 1])
            push(bottom, b_recv.at[g, ch, j * 4 + 3], down_b)

        @pl.when(k >= 12)
        def _():
            arrive(top, b_recv.at[g, ch, j * 4 + 2])
            arrive(bottom, b_recv.at[g, ch, j * 4 + 3])

        push(full, s_recv.at[g, ch, k], sibling)

    def arrive_other(g, ch, k, buf):
        ref = buf.at[ch, other_shard(k)]
        pltpu.make_async_remote_copy(
            src_ref=ref, dst_ref=ref, send_sem=ag_send.at[g, ch], recv_sem=s_recv.at[g, ch, k],
            device_id={"rank": sibling}, device_id_type=MESH,
        ).wait_recv()

    def out_part(ch, s):
        w = ow_v[pl.ds(pl.multiple_of(s * LANES, LANES), LANES), :]
        return jnp.dot(vbuf[ch, s], w, preferred_element_type=F32)

    def hidden_part(ch, s):
        x = mbuf[ch, s].astype(F32)
        squares = x * x
        ssq[ch] += squares[:, :128] + squares[:, 128:]
        xg = (x * gain_ref[pl.ds(s, 1), :]).astype(BF16)
        rows = pl.ds(pl.multiple_of(s * COLS, 32), LANES)
        accg[ch] += jnp.dot(xg, gw_v[rows, :], preferred_element_type=F32)
        accu[ch] += jnp.dot(xg, uw_v[rows, :], preferred_element_type=F32)

    def step(u, ch):
        @pl.when(u == 0)
        def _():
            own_ctx[ch].wait()
            pltpu.make_async_remote_copy(
                src_ref=sbuf.at[ch, pl.ds(0, N - 1)], dst_ref=cbuf.at[ch, pl.ds(0, N - 1)],
                send_sem=a2a_send.at[ch], recv_sem=a2a_recv.at[ch],
                device_id={"rank": sibling}, device_id_type=MESH,
            ).wait_recv()
            uv = jnp.concatenate([uv_v[0], uv_v[1]], axis=1)
            z = jnp.dot(cbuf[ch].reshape(N * 2 * SL, LAT), uv, preferred_element_type=F32)
            z = z.reshape(N, 2, SL, LANES)
            first = z[:, 0, :, :128].reshape(RC, 128)
            second = z[:, 1, :, 128:].reshape(RC, 128)
            vbuf[ch, me] = jnp.concatenate([first, second], axis=1).astype(BF16)

        @pl.when((u >= 0) & (u < 16))
        def _():
            action(0, ch, u, vbuf)

        @pl.when((u >= 1) & (u <= 16))
        def _():
            arrive_other(0, ch, u - 1, vbuf)
            acc[ch] += out_part(ch, shard(u - 1)) + out_part(ch, other_shard(u - 1))

        @pl.when(u == 16)
        def _():
            res = rr[...].astype(F32)[:, ch * SL : (ch + 1) * SL, :].reshape(RC, LANES)
            mbuf[ch, me] = jnp.zeros((RC, LANES), BF16)
            mbuf[ch, me, :, 0:COLS] = (res[:, 0:COLS] + acc[ch]).astype(BF16)

        @pl.when((u >= 16) & (u < 32))
        def _():
            action(1, ch, u - 16, mbuf)

        @pl.when((u >= 17) & (u <= 32))
        def _():
            arrive_other(1, ch, u - 17, mbuf)
            hidden_part(ch, shard(u - 17))
            hidden_part(ch, other_shard(u - 17))

    def body(t, carry):
        for ch in range(NC):
            step(t - ch * SKEW, ch)
        return carry

    lax.fori_loop(0, STEPS + (NC - 1) * SKEW, body, 0)

    pair = pl.ds(pl.multiple_of((me // 2) * 16, 16), 16)
    odd = core > 0
    for s in range(N):
        both = []
        for ch in range(NC):
            tile = mbuf[ch, s, pair, :].astype(F32)
            both.append(jnp.where(odd, tile[8:], tile[:8]))
        mixed_ref[:, s * COLS : (s + 1) * COLS] = jnp.concatenate(both, axis=0)[:, :COLS].astype(BF16)

    pieces = []
    for ch in range(NC):
        factor = lax.rsqrt(jnp.sum(ssq[ch], axis=1, keepdims=True) * (1.0 / D) + 1e-6)
        gate = accg[ch] * factor
        upper = accu[ch] * factor
        pieces.append((gate / (1.0 + jnp.exp(-gate)) * upper).reshape(N, SL, HID))
    activ_ref[...] = jnp.concatenate(pieces, axis=1).reshape(N * SLOTS, HID).astype(BF16)

    def sent(buf, sem):
        pltpu.make_async_remote_copy(
            src_ref=buf.at[pl.ds(0, N - 1)], dst_ref=buf.at[pl.ds(0, N - 1)], send_sem=sem, recv_sem=res_recv,
            device_id={"rank": sibling}, device_id_type=MESH,
        ).wait_send()

    for ch in range(NC):
        sent(sbuf.at[ch], a2a_send.at[ch])
        sent(vbuf.at[ch], ag_send.at[0, ch])
        sent(mbuf.at[ch], ag_send.at[1, ch])


def per_device(
    queries, cache_pool, lengths, block_table, residual, norm_gain, uv_weight, out_weight, gate_weight, up_weight
):
    gain = jnp.pad(norm_gain.reshape(N, COLS).astype(F32), ((0, 0), (0, LANES - COLS)))
    vmem = pl.BlockSpec(memory_space=pltpu.VMEM)
    smem = pl.BlockSpec(memory_space=pltpu.SMEM)
    hbm = pl.BlockSpec(memory_space=pl.ANY)
    dma = pltpu.SemaphoreType.DMA
    return pl.pallas_call(
        kernel,
        out_shape=(
            jax.ShapeDtypeStruct((SLOTS, D), BF16),
            jax.ShapeDtypeStruct((N * SLOTS, HID), BF16),
        ),
        in_specs=[smem, smem, hbm, hbm, hbm, vmem, hbm, hbm, hbm, hbm],
        out_specs=(vmem, vmem),
        scratch_shapes=[
            pltpu.VMEM((SLOTS, HEADS, WIDTH), BF16),
            pltpu.VMEM((SLOTS, PAGE, WIDTH), BF16),
            pltpu.VMEM((SLOTS, D), BF16),
            pltpu.VMEM((2, LAT, 128), BF16),
            pltpu.VMEM((N * LANES, COLS), BF16),
            pltpu.VMEM((D + 32, HID), BF16),
            pltpu.VMEM((D + 32, HID), BF16),
            pltpu.VMEM((SLOTS // 4, 4, TOK), F32),
            pltpu.VMEM((LAT // 128, SLOTS * HEADS, 128), F32),
            pltpu.VMEM((NC, N, 2 * SL, LAT), BF16),
            pltpu.VMEM((NC, N, 2 * SL, LAT), BF16),
            pltpu.VMEM((N, SLOTS, LANES), BF16),
            pltpu.VMEM((N, SLOTS, LANES), BF16),
            pltpu.VMEM((NC, N, RC, LANES), BF16),
            pltpu.VMEM((NC, N, RC, LANES), BF16),
            pltpu.VMEM((NC, RC, COLS), F32),
            pltpu.VMEM((NC, RC, HID), F32),
            pltpu.VMEM((NC, RC, HID), F32),
            pltpu.VMEM((NC, RC, 128), F32),
            dma((7,)),
            dma((NC + 1,)),
            dma,
            dma,
            dma((NC,)),
            dma((NC,)),
            dma((2, NC)),
            dma((2, NC, 4)),
            dma((2, NC, 16)),
            dma((2, NC, 16)),
        ],
        compiler_params=pltpu.CompilerParams(
            collective_id=0, has_side_effects=True, vmem_limit_bytes=60 * 1024 * 1024
        ),
        cost_estimate=pl.CostEstimate(flops=7 * 10**9, bytes_accessed=15 * 10**6, transcendentals=10**6),
    )(
        lengths, block_table, queries, cache_pool, residual, gain, uv_weight, out_weight, gate_weight, up_weight
    )


def solution(mesh):
    placed = (
        P(("group", "rank"), None, None),
        P(("group", "rank"), None, None),
        P(("group", "rank")),
        P(("group", "rank"), None),
        P(("group", "rank"), None),
        P(),
        P("rank", None, None),
        P(None, "rank"),
        P(None, "rank"),
        P(None, "rank"),
    )
    return jax.shard_map(
        per_device,
        mesh=mesh,
        in_specs=placed,
        out_specs=(P(("group", "rank"), None), P("group", "rank")),
        check_vma=False,
    )
```

time: 199 us -> 123 us (0.62)
  waiting for transfers between devices: 107 us -> 0 us
  Pallas kernels: 0 us -> 94.6 us
  blocking collectives: 38 us -> 0 us
  matrix products: 23.9 us -> 0 us
  local copies, waits for them, and re-layouts: 7.06 us -> 26.7 us
  between operations: 14.2 us -> 0.64 us
  starting transfers between devices: 5.73 us -> 0 us
  other arithmetic: 2.95 us -> 0.62 us
    all_gather x2 -> x0, waiting for transfers between devices: 98.2 us -> none  [the longest x1 54 us: per_device(): lax.all_gather(normed, 'rank', axis=0, tiled=True)]
    pallas_call x0 -> x1, Pallas kernels: none -> 94.6 us  [per_device(): pl.pallas_call(kernel, out_shape=(jax.ShapeDtypeStruct((SLOTS, D), BF16),...]
    all_to_all x2 -> x0, blocking collectives: 38 us -> none  [the longest x1 25.6 us: per_device(): lax.all_to_all(context, 'rank', split_axis=1, concat_axis=0, tiled=True)]
    dot_general x6 -> x0, matrix products: 23.9 us -> none  [the longest x1 6.73 us: gated_units(): gate = jnp.dot(normed, gate_weight, preferred_element_type=jnp.float32)]
    unnamed x14 -> x5, local copies, waits for them, and re-layouts: 0.8 us -> 24 us
    all_to_all x1 -> x0, waiting for transfers between devices: 8.65 us -> none  [per_device(): lax.all_to_all(mixed_cols, 'rank', split_axis=0, concat_axis=1, tiled=True)]
    all_to_all x1 -> x0, starting transfers between devices: 5.47 us -> none  [per_device(): lax.all_to_all(mixed_cols, 'rank', split_axis=0, concat_axis=1, tiled=True)]
    gather x1 -> x0, local copies, waits for them, and re-layouts: 3.44 us -> none  [attend(): keys_all = cache_pool[block_table].reshape(slots, -1, width)]
  transfers between devices with their start and end apart: 3 -> 0, of which waited for: 3 -> 0; matrix products, arithmetic and copies ran while one was open for 0% -> 0% of each run, Pallas kernels for 0% -> 0%
where the time goes in v1:
time: 123 us
  Pallas kernels  94.6 us (77%)
  local copies, waits for them, and re-layouts  26.7 us (22%)
    pallas_call x1, Pallas kernels, per_device(): pl.pallas_call(kernel, out_shape=(jax.ShapeDtypeStruct((SLOTS, D), BF16),...  94.6 us
    unnamed x5, local copies, waits for them, and re-layouts  24 us

profile of v1, /device:TPU:1, one launch (start us, length us, event | category | flops | bytes accessed | tf_op | source)
XLA Modules:
  0.0 122.5 jit_solution(13622822753772726890)
XLA Ops:
  0.6 1.4 %copy.12.bt_ref = s32[16,4]{1,0:T(8,128)} copy(s32[16,4]{0,1:T(4,128)} %param.13) | data formatting | bytes 512 | tf_op args[3]
  2.0 0.8 convert_element_type.6
  2.8 0.6 pad_convert_fusion.gain_ref
  3.4 6.3 %copy.13.ow_hbm = bf16[8192,224]{1,0:T(8,128)(2,1)} copy(bf16[8192,224]{0,1:T(8,128)(2,1)} %param.17) | data formatting | bytes 7340032 | tf_op args[7]
  9.7 7.4 %copy.14.gw_hbm = bf16[7168,288]{1,0:T(8,128)(2,1)} copy(bf16[7168,288]{0,1:T(8,128)(2,1)} %param.18) | data formatting | bytes 8257536 | tf_op args[8]
  17.1 7.4 %copy.15.uw_hbm = bf16[7168,288]{1,0:T(8,128)(2,1)} copy(bf16[7168,288]{0,1:T(8,128)(2,1)} %param.19) | data formatting | bytes 8257536 | tf_op args[9]
  24.4 94.6 %shard_map.113 = (bf16[16,7168]{1,0:T(8,128)(2,1)}, bf16[512,288]{1,0:T(8,128)(2,1)}) custom-call(s32[16]{0:T(128)} %len_ref.1, s32[16,4]{1,0:T(8,128)} %copy.12.bt_ref, bf16[16,64,576]{2,1,0:T(8,128)(2,1)} %q_hbm.1, bf16[16,32,576]{2,1,0:T(8,128)(2,1)} %pool_hbm.1, bf16[16,7168]{1,0:T(8,128)(2,1)} %res_hbm.1, f32[32,256]{1,0:T(8,128)} %pad_convert_fusion.gain_ref, ...), custom_call_target="tpu_custom_call" | custom-call | flops 7000000000 | bytes 15000000 | tf_op jit(solution)/shard_map/pallas_call | solution.py:365
  119.0 1.9 %copy.16 = bf16[512,288]{0,1:T(8,128)(2,1)} copy(bf16[512,288]{1,0:T(8,128)(2,1)} %get-tuple-element.3) | data formatting | bytes 589824 | tf_op jit(solution)/shard_map/pallas_call | solution.py:365
  120.9 1.6 %copy.18 = bf16[16,7168]{1,0:T(8,128)(2,1)} copy(bf16[16,7168]{1,0:T(8,128)(2,1)} %get-tuple-element.6) | data formatting | bytes 458752

commit v2 on v1

v2 whole, which is shorter than its diff:
```python
import jax
import jax.numpy as jnp
from jax import lax
from jax.experimental import pallas as pl
from jax.experimental.pallas import tpu as pltpu
from jax.sharding import PartitionSpec as P

F32 = jnp.float32
BF16 = jnp.bfloat16
MESH = pl.DeviceIdType.MESH

N = 32
SLOTS = 16
HEADS = 64
LAT = 512
WIDTH = 576
TOK = 512
PAGE = 32
MAXP = 4
D = 7168
COLS = 224
HID = 288
LANES = 256

NC = 2
SL = SLOTS // NC
RC = N * SL

FULL, TOP, BOTTOM = range(3)

score_scale = 192.0 ** (-0.5)


def kernel(
    len_ref, bt_ref, q_hbm, pool_hbm, res_hbm, gain_hbm, uv_hbm, ow_hbm, gw_hbm, uw_hbm,
    mixed_ref, activ_ref,
    q_v, pool_v, res_v, uv_v, ow_v, gw_v, uw_v,
    gain_v, gain_w, mask_v, ctx, sbuf, cbuf, rs, rr, vbuf, mbuf, wp, acc, hid, ssq, picked, own_rows, order, out,
    load_sem, own_sem, res_send, res_recv, a2a_send, a2a_recv, ag_send, a_recv, b_recv, s_recv,
):
    me = lax.axis_index("rank")
    core = me % 2
    xx = (me // 2) % 4
    yy = me // 8
    sa = (1 - core) * 2 + core * 8
    sb = (1 - core) * 8 + core * 2
    a = (1 - core) * xx + core * yy
    b = (1 - core) * yy + core * xx
    sibling = me + 1 - 2 * core

    def rank_at(pa, pb):
        return pa * sa + pb * sb + core

    up_a, down_a = rank_at((a + 1) % 4, b), rank_at((a + 3) % 4, b)
    up_b, down_b = rank_at(a, (b + 1) % 4), rank_at(a, (b + 3) % 4)

    barrier = pltpu.get_barrier_semaphore()

    def greet(k, carry):
        pl.semaphore_signal(barrier, inc=1, device_id={"rank": (me + k) % N}, device_id_type=MESH)
        return carry

    lax.fori_loop(1, N, greet, 0)

    loads = [
        pltpu.make_async_copy(src, dst, load_sem.at[i])
        for i, (src, dst) in enumerate(
            [
                (q_hbm, q_v),
                (pool_hbm, pool_v),
                (res_hbm, res_v),
                (uv_hbm, uv_v),
                (ow_hbm, ow_v),
                (gw_hbm, gw_v),
                (uw_hbm, uw_v),
                (gain_hbm, gain_v),
            ]
        )
    ]
    for load in loads:
        load.start()

    lane = lax.broadcasted_iota(jnp.int32, (1, TOK), 1)
    page_of = lane // PAGE
    offset = lane % PAGE
    for slot in range(SLOTS):
        n = len_ref[slot]
        valid = jnp.zeros((1, TOK), F32)
        for m in range(MAXP):
            hit = (page_of == bt_ref[m, slot]) & (offset + m * PAGE < n)
            valid = jnp.where(hit, 1.0, valid)
        mask_v[slot // 4, slot % 4 : slot % 4 + 1, :] = valid
    hid[...] = jnp.zeros_like(hid)
    ssq[...] = jnp.zeros_like(ssq)
    row = lax.broadcasted_iota(jnp.int32, (NC * RC, NC * RC), 0)
    col = lax.broadcasted_iota(jnp.int32, (NC * RC, NC * RC), 1)
    home = (row % RC) // SL * SLOTS + row // RC * SL + row % SL
    order[...] = jnp.where(home == col, 1.0, 0.0).astype(BF16)
    for ch in range(NC):
        slot = lax.broadcasted_iota(jnp.int32, (SLOTS, RC), 0)
        col = lax.broadcasted_iota(jnp.int32, (SLOTS, RC), 1)
        hit = (slot // SL == ch) & (col == me * SL + slot % SL)
        own_rows[ch] = jnp.where(hit, 1.0, 0.0).astype(BF16)

    loads[0].wait()
    loads[1].wait()

    def dest_of(k):
        p = (k * 11) % N
        return ((yy + p // 8) % 4) * 8 + ((xx + (p // 2) % 4) % 4) * 2 + (core + p % 2) % 2

    def attend(first, carry):
        q = q_v[pl.ds(first * 4, 4)].reshape(4 * HEADS, WIDTH)
        scores = lax.dot_general(
            q, pool_v[...].reshape(TOK, WIDTH), (((1,), (1,)), ((), ())), preferred_element_type=F32
        ) * score_scale
        ok = jnp.broadcast_to(
            mask_v[first][:, None, :], (4, HEADS, TOK)
        ).reshape(4 * HEADS, TOK) > 0.0
        scores = jnp.where(ok, scores, -1e30)
        peak = jnp.max(scores, axis=1, keepdims=True)
        expo = jnp.where(ok, jnp.exp(scores - peak), 0.0)
        total = jnp.sum(expo, axis=1, keepdims=True)
        total = jnp.where(total > 0.0, total, 1.0)
        weights = (expo / total).astype(BF16)
        out = jnp.dot(weights, pool_v[...].reshape(TOK, WIDTH)[:, :LAT], preferred_element_type=F32)
        for part in range(LAT // 128):
            ctx[part, pl.ds(pl.multiple_of(first * 4 * HEADS, 4 * HEADS), 4 * HEADS), :] = out[
                :, part * 128 : (part + 1) * 128
            ]
        return carry

    own_ctx = []
    for ch in range(NC):
        lax.fori_loop(ch * SL // 4, (ch + 1) * SL // 4, attend, 0)

        def pack(r, carry, ch=ch):
            for part in range(LAT // 128):
                pair = [
                    ctx[part, pl.ds(ch * SL * HEADS + 2 * r + h, SL, stride=HEADS), :] for h in range(2)
                ]
                sbuf[ch, r, :, part * 128 : (part + 1) * 128] = jnp.concatenate(pair, axis=0).astype(BF16)
            return carry

        lax.fori_loop(0, N, pack, 0)

        if ch == 0:
            pl.semaphore_wait(barrier, N - 1)

        def send_ctx(k, carry, ch=ch):
            to = dest_of(k)
            pltpu.make_async_remote_copy(
                src_ref=sbuf.at[ch, to], dst_ref=cbuf.at[ch, me],
                send_sem=a2a_send.at[ch], recv_sem=a2a_recv.at[ch],
                device_id={"rank": to}, device_id_type=MESH,
            ).start()
            return carry

        lax.fori_loop(1, N, send_ctx, 0)
        own_ctx.append(pltpu.make_async_copy(sbuf.at[ch, me], cbuf.at[ch, me], own_sem.at[ch]))
        own_ctx[ch].start()

    loads[2].wait()
    for r in range(N):
        rs[r, :, 0:COLS] = res_v[:, r * COLS : (r + 1) * COLS]
        rs[r, :, COLS:LANES] = jnp.zeros((SLOTS, LANES - COLS), BF16)

    def send_res(k, carry):
        to = dest_of(k)
        pltpu.make_async_remote_copy(
            src_ref=rs.at[to], dst_ref=rr.at[me], send_sem=res_send, recv_sem=res_recv,
            device_id={"rank": to}, device_id_type=MESH,
        ).start()
        return carry

    lax.fori_loop(1, N, send_res, 0)
    own_res = pltpu.make_async_copy(rs.at[me], rr.at[me], own_sem.at[NC])
    own_res.start()

    for load in loads[3:]:
        load.wait()

    gain_w[...] = gain_v[...].astype(F32)

    def align(q, carry):
        lanes = pl.ds(pl.multiple_of(q * 4 * COLS, 128), 4 * COLS)
        gain = jnp.concatenate([gain_w[pl.ds(q * 7 + i, 1), :] for i in range(7)], axis=1)
        for first, w in ((0, gw_v), (HID, uw_v)):
            scaled = (w[:, lanes].astype(F32) * gain).astype(BF16)
            for i in range(4):
                wp[q * 4 + i, first : first + HID, :] = scaled[:, i * COLS : (i + 1) * COLS]
        return carry

    lax.fori_loop(0, N // 4, align, 0)

    def turn(j):
        return (4 - j + (j // 2) * 3 + (j // 3) * 2) % 4

    def shard(j, i):
        return rank_at((a + turn(j)) % 4, (b + turn(i)) % 4)

    def other_shard(j, i):
        return ((b + turn(j)) % 4) * sb + ((a + turn(i)) % 4) * sa + (1 - core)

    bufs = (vbuf, mbuf)

    def piece(g, ch, s, part):
        buf = bufs[g]
        half = buf.shape[2] // 2
        if part == FULL:
            return buf.at[ch, s]
        return buf.at[ch, s, pl.ds(0 if part == TOP else half, half)]

    def push(g, ch, ref, sem, to):
        pltpu.make_async_remote_copy(
            src_ref=ref, dst_ref=ref, send_sem=ag_send.at[g, ch], recv_sem=sem,
            device_id={"rank": to}, device_id_type=MESH,
        ).start()

    def arrive(g, ch, ref, sem):
        pltpu.make_async_remote_copy(
            src_ref=ref, dst_ref=ref, send_sem=ag_send.at[g, ch], recv_sem=sem,
            device_id={"rank": sibling}, device_id_type=MESH,
        ).wait_recv()

    def share(g, ch, j, i):
        push(g, ch, piece(g, ch, shard(j, i), FULL), s_recv.at[g, ch, j * 4 + i], sibling)

    def along_b(g, ch, j):
        full = piece(g, ch, shard(j, 0), FULL)
        push(g, ch, full, b_recv.at[g, ch, j * 4], up_b)
        push(g, ch, full, b_recv.at[g, ch, j * 4 + 1], down_b)
        share(g, ch, j, 0)

    def open_line(g, ch):
        own = piece(g, ch, me, FULL)
        push(g, ch, own, a_recv.at[g, ch, 0], up_a)
        push(g, ch, own, a_recv.at[g, ch, 1], down_a)
        along_b(g, ch, 0)

    def own_line(g, ch):
        s = shard(1, 0)
        arrive(g, ch, piece(g, ch, s, FULL), a_recv.at[g, ch, 0])
        push(g, ch, piece(g, ch, s, TOP), a_recv.at[g, ch, 2], up_a)
        along_b(g, ch, 1)
        s = shard(2, 0)
        arrive(g, ch, piece(g, ch, s, FULL), a_recv.at[g, ch, 1])
        push(g, ch, piece(g, ch, s, BOTTOM), a_recv.at[g, ch, 3], down_a)
        along_b(g, ch, 2)
        s = shard(3, 0)
        arrive(g, ch, piece(g, ch, s, TOP), a_recv.at[g, ch, 2])
        arrive(g, ch, piece(g, ch, s, BOTTOM), a_recv.at[g, ch, 3])
        along_b(g, ch, 3)

    def next_lines(g, ch, j):
        s = shard(j, 1)
        arrive(g, ch, piece(g, ch, s, FULL), b_recv.at[g, ch, j * 4])
        push(g, ch, piece(g, ch, s, TOP), b_recv.at[g, ch, j * 4 + 2], up_b)
        share(g, ch, j, 1)
        s = shard(j, 2)
        arrive(g, ch, piece(g, ch, s, FULL), b_recv.at[g, ch, j * 4 + 1])
        push(g, ch, piece(g, ch, s, BOTTOM), b_recv.at[g, ch, j * 4 + 3], down_b)
        share(g, ch, j, 2)

    def last_line(g, ch, j):
        s = shard(j, 3)
        arrive(g, ch, piece(g, ch, s, TOP), b_recv.at[g, ch, j * 4 + 2])
        arrive(g, ch, piece(g, ch, s, BOTTOM), b_recv.at[g, ch, j * 4 + 3])
        share(g, ch, j, 3)

    def out_part(ch, s):
        w = ow_v[:, pl.ds(pl.multiple_of(s * LANES, LANES), LANES)]
        return lax.dot_general(w, vbuf[ch, s], (((1,), (1,)), ((), ())), preferred_element_type=F32)

    def hidden_part(ch, s):
        x = mbuf[ch, s]
        wide = x.astype(F32)
        ssq[ch] += jnp.sum((wide * wide).reshape(COLS // 8, 8, RC), axis=0)
        picked[ch, s] = lax.dot_general(own_rows[ch], x, (((1,), (1,)), ((), ())), preferred_element_type=F32)
        return jnp.dot(wp[s], x, preferred_element_type=F32)

    def compute(g, ch, j, lines):
        total, part = ((acc, out_part), (hid, hidden_part))[g]
        for i in lines:
            arrive(g, ch, piece(g, ch, other_shard(j, i), FULL), s_recv.at[g, ch, j * 4 + i])
        total[ch] += sum(part(ch, s(j, i)) for i in lines for s in (shard, other_shard))

    def item(n):
        ch = (n + 3) // 8 + (n + 7) // 8 - (n + 6) // 8
        j = ((n + 6) // 8) * (n - 1) - 3 * ((n + 3) // 8)
        return ch, j

    def gather(g, finish):
        for ch in range(NC):
            own_line(g, ch)

        def middle(n, carry):
            next_lines(g, *item(n))
            compute(g, *item(n), (0,))

            @pl.when(n > 0)
            def _():
                compute(g, *item(n - 1), (1, 2))

            return carry

        lax.fori_loop(0, 8, middle, 0)
        last_line(g, *item(0))
        compute(g, *item(7), (1, 2))

        def ending(n, carry):
            last_line(g, *item(n))
            compute(g, *item(n - 1), (3,))
            return carry

        lax.fori_loop(1, 5, ending, 0)
        compute(g, *item(4), (3,))
        finish(0)
        last_line(g, *item(5))
        lax.fori_loop(6, 8, ending, 0)
        compute(g, *item(7), (3,))
        finish(1)

    for ch in range(NC):
        own_ctx[ch].wait()
        pltpu.make_async_remote_copy(
            src_ref=sbuf.at[ch, pl.ds(0, N - 1)], dst_ref=cbuf.at[ch, pl.ds(0, N - 1)],
            send_sem=a2a_send.at[ch], recv_sem=a2a_recv.at[ch],
            device_id={"rank": sibling}, device_id_type=MESH,
        ).wait_recv()
        uv = jnp.concatenate([uv_v[0], uv_v[1]], axis=1)
        z = jnp.dot(cbuf[ch].reshape(N * 2 * SL, LAT), uv, preferred_element_type=F32)
        z = z.reshape(N, 2, SL, LANES)
        first = z[:, 0, :, :128].reshape(RC, 128)
        second = z[:, 1, :, 128:].reshape(RC, 128)
        vbuf[ch, me] = jnp.concatenate([first, second], axis=1).astype(BF16)
        open_line(0, ch)

    own_res.wait()
    pltpu.make_async_remote_copy(
        src_ref=rs.at[pl.ds(0, N - 1)], dst_ref=rr.at[pl.ds(0, N - 1)], send_sem=res_send, recv_sem=res_recv,
        device_id={"rank": sibling}, device_id_type=MESH,
    ).wait()
    for ch in range(NC):
        res = rr[...].astype(F32)[:, ch * SL : (ch + 1) * SL, :].reshape(RC, LANES)
        acc[ch] = res.T[:COLS]

    def mix(ch):
        mbuf[ch, me] = acc[ch].astype(BF16)
        open_line(1, ch)

    def finish(ch):
        factor = lax.rsqrt(jnp.sum(ssq[ch], axis=0, keepdims=True) * (1.0 / D) + 1e-6)
        gate = hid[ch, :HID] * factor
        upper = hid[ch, HID:] * factor
        activ = (gate / (1.0 + jnp.exp(-gate)) * upper).astype(BF16)
        out[ch] = jnp.dot(activ, order[ch * RC : (ch + 1) * RC, :], preferred_element_type=F32)

    gather(0, mix)
    gather(1, finish)

    for s in range(N):
        rows = picked[0, s]
        for ch in range(1, NC):
            rows += picked[ch, s]
        mixed_ref[:, s * COLS : (s + 1) * COLS] = rows.astype(BF16)

    activ_ref[...] = (out[0] + out[1]).astype(BF16)

    def sent(buf, sem):
        pltpu.make_async_remote_copy(
            src_ref=buf.at[pl.ds(0, N - 1)], dst_ref=buf.at[pl.ds(0, N - 1)], send_sem=sem, recv_sem=res_recv,
            device_id={"rank": sibling}, device_id_type=MESH,
        ).wait_send()

    for ch in range(NC):
        sent(sbuf.at[ch], a2a_send.at[ch])
        sent(vbuf.at[ch], ag_send.at[0, ch])
        sent(mbuf.at[ch], ag_send.at[1, ch])


def hand_out(mixed_in, activ_in, mixed_out, activ_out, sem):
    copies = [
        pltpu.make_async_copy(mixed_in, mixed_out, sem.at[0]),
        pltpu.make_async_copy(activ_in, activ_out, sem.at[1]),
    ]
    for copy in copies:
        copy.start()
    for copy in copies:
        copy.wait()


def per_device(
    queries, cache_pool, lengths, block_table, residual, norm_gain, uv_weight, out_weight, gate_weight, up_weight
):
    gain = norm_gain.reshape(D // 128, 128)
    vmem = pl.BlockSpec(memory_space=pltpu.VMEM)
    smem = pl.BlockSpec(memory_space=pltpu.SMEM)
    hbm = pl.BlockSpec(memory_space=pl.ANY)
    dma = pltpu.SemaphoreType.DMA
    mixed, activ = pl.pallas_call(
        kernel,
        out_shape=(
            jax.ShapeDtypeStruct((SLOTS, D), BF16),
            jax.ShapeDtypeStruct((HID, N * SLOTS), BF16),
        ),
        in_specs=[smem, smem] + [hbm] * 8,
        out_specs=(vmem, vmem),
        scratch_shapes=[
            pltpu.VMEM((SLOTS, HEADS, WIDTH), BF16),
            pltpu.VMEM((SLOTS, PAGE, WIDTH), BF16),
            pltpu.VMEM((SLOTS, D), BF16),
            pltpu.VMEM((2, LAT, 128), BF16),
            pltpu.VMEM((COLS, N * LANES), BF16),
            pltpu.VMEM((HID, D), BF16),
            pltpu.VMEM((HID, D), BF16),
            pltpu.VMEM((D // 128, 128), BF16),
            pltpu.VMEM((D // 128, 128), F32),
            pltpu.VMEM((SLOTS // 4, 4, TOK), F32),
            pltpu.VMEM((LAT // 128, SLOTS * HEADS, 128), F32),
            pltpu.VMEM((NC, N, 2 * SL, LAT), BF16),
            pltpu.VMEM((NC, N, 2 * SL, LAT), BF16),
            pltpu.VMEM((N, SLOTS, LANES), BF16),
            pltpu.VMEM((N, SLOTS, LANES), BF16),
            pltpu.VMEM((NC, N, RC, LANES), BF16),
            pltpu.VMEM((NC, N, COLS, RC), BF16),
            pltpu.VMEM((N, 2 * HID, COLS), BF16),
            pltpu.VMEM((NC, COLS, RC), F32),
            pltpu.VMEM((NC, 2 * HID, RC), F32),
            pltpu.VMEM((NC, 8, RC), F32),
            pltpu.VMEM((NC, N, SLOTS, COLS), F32),
            pltpu.VMEM((NC, SLOTS, RC), BF16),
            pltpu.VMEM((NC * RC, NC * RC), BF16),
            pltpu.VMEM((NC, HID, NC * RC), F32),
            dma((8,)),
            dma((NC + 1,)),
            dma,
            dma,
            dma((NC,)),
            dma((NC,)),
            dma((2, NC)),
            dma((2, NC, 4)),
            dma((2, NC, 16)),
            dma((2, NC, 16)),
        ],
        compiler_params=pltpu.CompilerParams(
            collective_id=0, has_side_effects=True, vmem_limit_bytes=60 * 1024 * 1024
        ),
        cost_estimate=pl.CostEstimate(flops=7 * 10**9, bytes_accessed=15 * 10**6, transcendentals=10**6),
    )(
        lengths, block_table.T, queries, cache_pool, residual, gain, uv_weight,
        out_weight.T, gate_weight.T, up_weight.T,
    )
    mixed, activ = pl.pallas_call(
        hand_out,
        out_shape=(
            jax.ShapeDtypeStruct((SLOTS, D), BF16),
            jax.ShapeDtypeStruct((HID, N * SLOTS), BF16),
        ),
        in_specs=[vmem, vmem],
        out_specs=(hbm, hbm),
        scratch_shapes=[dma((2,))],
    )(mixed, activ)
    return mixed, activ.T


def solution(mesh):
    placed = (
        P(("group", "rank"), None, None),
        P(("group", "rank"), None, None),
        P(("group", "rank")),
        P(("group", "rank"), None),
        P(("group", "rank"), None),
        P(),
        P("rank", None, None),
        P(None, "rank"),
        P(None, "rank"),
        P(None, "rank"),
    )
    return jax.shard_map(
        per_device,
        mesh=mesh,
        in_specs=placed,
        out_specs=(P(("group", "rank"), None), P("group", "rank")),
        check_vma=False,
    )
```

time: 123 us -> 81.8 us (0.67)
  local copies, waits for them, and re-layouts: 26.7 us -> 0 us
  Pallas kernels: 94.6 us -> 81.1 us
    unnamed x5 -> x0, local copies, waits for them, and re-layouts: 24 us -> none
    pallas_call x1, Pallas kernels: 94.6 us -> 79.2 us  [per_device(): pl.pallas_call(kernel, out_shape=(jax.ShapeDtypeStruct((SLOTS, D), BF16),...]
    pallas_call x0 -> x1, Pallas kernels: none -> 1.89 us  [per_device(): pl.pallas_call(hand_out, out_shape=(jax.ShapeDtypeStruct((SLOTS, D), BF16...]
    pallas_call x1 -> x0, local copies, waits for them, and re-layouts: 1.86 us -> none  [per_device(): pl.pallas_call(kernel, out_shape=(jax.ShapeDtypeStruct((SLOTS, D), BF16),...]
where the time goes in v2:
time: 81.8 us; the launch traced here: 81.7 us
  Pallas kernels  81.1 us (99%)
    pallas_call x1, Pallas kernels, per_device(): pl.pallas_call(kernel, out_shape=(jax.ShapeDtypeStruct((SLOTS, D), BF16),...  79.2 us
    pallas_call x1, Pallas kernels, per_device(): pl.pallas_call(hand_out, out_shape=(jax.ShapeDtypeStruct((SLOTS, D), BF16...  1.89 us

profile of v2, /device:TPU:1, one launch (start us, length us, event | category | flops | bytes accessed | tf_op | source)
XLA Modules:
  0.0 81.7 jit_solution(14855070486613152931)
XLA Ops:
  0.6 79.2 %shard_map.113 = (bf16[16,7168]{1,0:T(8,128)(2,1)}, bf16[288,512]{1,0:T(8,128)(2,1)}) custom-call(s32[16]{0:T(128)} %len_ref.1, s32[4,16]{1,0:T(4,128)} %bitcast.11, bf16[16,64,576]{2,1,0:T(8,128)(2,1)} %q_hbm.1, bf16[16,32,576]{2,1,0:T(8,128)(2,1)} %pool_hbm.1, bf16[16,7168]{1,0:T(8,128)(2,1)} %res_hbm.1, bf16[56,128]{1,0:T(8,128)(2,1)} %bitcast.10, ...), custom_call_target="tpu_custom_call" | custom-call | flops 7000000000 | bytes 15000000 | tf_op jit(solution)/shard_map/pallas_call | solution.py:401
  79.8 1.9 %shard_map.114 = (bf16[16,7168]{1,0:T(8,128)(2,1)}, bf16[288,512]{1,0:T(8,128)(2,1)}) custom-call(bf16[16,7168]{1,0:T(8,128)(2,1)} %get-tuple-element.6.mixed_in, bf16[288,512]{1,0:T(8,128)(2,1)} %get-tuple-element.7.activ_in), custom_call_target="tpu_custom_call" | custom-call | tf_op jit(solution)/shard_map/pallas_call | solution.py:454

commit v3 on v2

--- a/solution.py
+++ b/solution.py
@@ -27,6 +27,17 @@
 RC = N * SL
 
 FULL, TOP, BOTTOM = range(3)
+
+ORDER = (
+    ("o1", "o2"),
+    ("d0", "c10", "u0", "c20", "c00", "c02", "c01", "o3"),
+    ("d1", "u1", "u2", "d2", "c30"),
+    ("c11", "c22", "l0", "c21"),
+    ("d3", "u3", "c12", "c03"),
+    ("c32", "l1", "c31"),
+    ("l2", "c13", "l3"),
+    ("c23", "c33"),
+)
 
 score_scale = 192.0 ** (-0.5)
 
@@ -90,6 +101,7 @@
             hit = (page_of == bt_ref[m, slot]) & (offset + m * PAGE < n)
             valid = jnp.where(hit, 1.0, valid)
         mask_v[slot // 4, slot % 4 : slot % 4 + 1, :] = valid
+    acc[...] = jnp.zeros_like(acc)
     hid[...] = jnp.zeros_like(hid)
     ssq[...] = jnp.zeros_like(ssq)
     row = lax.broadcasted_iota(jnp.int32, (NC * RC, NC * RC), 0)
@@ -238,25 +250,26 @@
         push(g, ch, own, a_recv.at[g, ch, 1], down_a)
         along_b(g, ch, 0)
 
-    def own_line(g, ch):
-        s = shard(1, 0)
-        arrive(g, ch, piece(g, ch, s, FULL), a_recv.at[g, ch, 0])
-        push(g, ch, piece(g, ch, s, TOP), a_recv.at[g, ch, 2], up_a)
-        along_b(g, ch, 1)
-        s = shard(2, 0)
-        arrive(g, ch, piece(g, ch, s, FULL), a_recv.at[g, ch, 1])
-        push(g, ch, piece(g, ch, s, BOTTOM), a_recv.at[g, ch, 3], down_a)
-        along_b(g, ch, 2)
-        s = shard(3, 0)
-        arrive(g, ch, piece(g, ch, s, TOP), a_recv.at[g, ch, 2])
-        arrive(g, ch, piece(g, ch, s, BOTTOM), a_recv.at[g, ch, 3])
-        along_b(g, ch, 3)
-
-    def next_lines(g, ch, j):
+    def own_line(g, ch, j):
+        s = shard(j, 0)
+        if j == 1:
+            arrive(g, ch, piece(g, ch, s, FULL), a_recv.at[g, ch, 0])
+            push(g, ch, piece(g, ch, s, TOP), a_recv.at[g, ch, 2], up_a)
+        elif j == 2:
+            arrive(g, ch, piece(g, ch, s, FULL), a_recv.at[g, ch, 1])
+            push(g, ch, piece(g, ch, s, BOTTOM), a_recv.at[g, ch, 3], down_a)
+        else:
+            arrive(g, ch, piece(g, ch, s, TOP), a_recv.at[g, ch, 2])
+            arrive(g, ch, piece(g, ch, s, BOTTOM), a_recv.at[g, ch, 3])
+        along_b(g, ch, j)
+
+    def line_below(g, ch, j):
         s = shard(j, 1)
         arrive(g, ch, piece(g, ch, s, FULL), b_recv.at[g, ch, j * 4])
         push(g, ch, piece(g, ch, s, TOP), b_recv.at[g, ch, j * 4 + 2], up_b)
         share(g, ch, j, 1)
+
+    def line_above(g, ch, j):
         s = shard(j, 2)
         arrive(g, ch, piece(g, ch, s, FULL), b_recv.at[g, ch, j * 4 + 1])
         push(g, ch, piece(g, ch, s, BOTTOM), b_recv.at[g, ch, j * 4 + 3], down_b)
@@ -279,47 +292,34 @@
         picked[ch, s] = lax.dot_general(own_rows[ch], x, (((1,), (1,)), ((), ())), preferred_element_type=F32)
         return jnp.dot(wp[s], x, preferred_element_type=F32)
 
-    def compute(g, ch, j, lines):
+    def compute(g, ch, j, i):
         total, part = ((acc, out_part), (hid, hidden_part))[g]
-        for i in lines:
-            arrive(g, ch, piece(g, ch, other_shard(j, i), FULL), s_recv.at[g, ch, j * 4 + i])
-        total[ch] += sum(part(ch, s(j, i)) for i in lines for s in (shard, other_shard))
-
-    def item(n):
-        ch = (n + 3) // 8 + (n + 7) // 8 - (n + 6) // 8
-        j = ((n + 6) // 8) * (n - 1) - 3 * ((n + 3) // 8)
-        return ch, j
-
-    def gather(g, finish):
-        for ch in range(NC):
-            own_line(g, ch)
-
-        def middle(n, carry):
-            next_lines(g, *item(n))
-            compute(g, *item(n), (0,))
-
-            @pl.when(n > 0)
-            def _():
-                compute(g, *item(n - 1), (1, 2))
-
-            return carry
-
-        lax.fori_loop(0, 8, middle, 0)
-        last_line(g, *item(0))
-        compute(g, *item(7), (1, 2))
-
-        def ending(n, carry):
-            last_line(g, *item(n))
-            compute(g, *item(n - 1), (3,))
-            return carry
-
-        lax.fori_loop(1, 5, ending, 0)
-        compute(g, *item(4), (3,))
-        finish(0)
-        last_line(g, *item(5))
-        lax.fori_loop(6, 8, ending, 0)
-        compute(g, *item(7), (3,))
-        finish(1)
+        arrive(g, ch, piece(g, ch, other_shard(j, i), FULL), s_recv.at[g, ch, j * 4 + i])
+        total[ch] += part(ch, shard(j, i)) + part(ch, other_shard(j, i))
+
+    acts = {"o": own_line, "d": line_below, "u": line_above, "l": last_line}
+
+    def stage(g, ch, work):
+        for name in work:
+            if name[0] == "c":
+                compute(g, ch, int(name[1]), int(name[2]))
+            else:
+                acts[name[0]](g, ch, int(name[1]))
+
+    def gather(g, early, finish):
+        for n, work in enumerate(ORDER):
+            def body(ch, carry, work=work):
+                stage(g, ch, work)
+                return carry
+
+            if n < len(ORDER) - 1:
+                lax.fori_loop(0, NC, body, 0)
+            else:
+                for ch in range(NC):
+                    stage(g, ch, work)
+                    finish(ch)
+            if n == 0:
+                early()
 
     for ch in range(NC):
         own_ctx[ch].wait()
@@ -336,14 +336,15 @@
         vbuf[ch, me] = jnp.concatenate([first, second], axis=1).astype(BF16)
         open_line(0, ch)
 
-    own_res.wait()
-    pltpu.make_async_remote_copy(
-        src_ref=rs.at[pl.ds(0, N - 1)], dst_ref=rr.at[pl.ds(0, N - 1)], send_sem=res_send, recv_sem=res_recv,
-        device_id={"rank": sibling}, device_id_type=MESH,
-    ).wait()
-    for ch in range(NC):
-        res = rr[...].astype(F32)[:, ch * SL : (ch + 1) * SL, :].reshape(RC, LANES)
-        acc[ch] = res.T[:COLS]
+    def add_residual():
+        own_res.wait()
+        pltpu.make_async_remote_copy(
+            src_ref=rs.at[pl.ds(0, N - 1)], dst_ref=rr.at[pl.ds(0, N - 1)], send_sem=res_send, recv_sem=res_recv,
+            device_id={"rank": sibling}, device_id_type=MESH,
+        ).wait()
+        for ch in range(NC):
+            res = rr[...].astype(F32)[:, ch * SL : (ch + 1) * SL, :].reshape(RC, LANES)
+            acc[ch] += res.T[:COLS]
 
     def mix(ch):
         mbuf[ch, me] = acc[ch].astype(BF16)
@@ -356,8 +357,8 @@
         activ = (gate / (1.0 + jnp.exp(-gate)) * upper).astype(BF16)
         out[ch] = jnp.dot(activ, order[ch * RC : (ch + 1) * RC, :], preferred_element_type=F32)
 
-    gather(0, mix)
-    gather(1, finish)
+    gather(0, add_residual, mix)
+    gather(1, lambda: None, finish)
 
     for s in range(N):
         rows = picked[0, s]
@@ -400,10 +401,7 @@
     dma = pltpu.SemaphoreType.DMA
     mixed, activ = pl.pallas_call(
         kernel,
-        out_shape=(
-            jax.ShapeDtypeStruct((SLOTS, D), BF16),
-            jax.ShapeDtypeStruct((HID, N * SLOTS), BF16),
-        ),
+        out_shape=(pltpu.VMEM((SLOTS, D), BF16), pltpu.VMEM((HID, N * SLOTS), BF16)),
         in_specs=[smem, smem] + [hbm] * 8,
         out_specs=(vmem, vmem),
         scratch_shapes=[
@@ -460,7 +458,7 @@
         in_specs=[vmem, vmem],
         out_specs=(hbm, hbm),
         scratch_shapes=[dma((2,))],
-    )(mixed, activ)
+    )(pltpu.with_memory_space_constraint(mixed, pltpu.VMEM), pltpu.with_memory_space_constraint(activ, pltpu.VMEM))
     return mixed, activ.T
 
 

time: 81.8 us -> 74 us (0.905)
  Pallas kernels: 81.1 us -> 73.2 us
    pallas_call x1, Pallas kernels: 79.2 us -> 72.4 us  [per_device(): pl.pallas_call(kernel, out_shape=(pltpu.VMEM((SLOTS, D), BF16), pltpu.VME...]
    pallas_call x1, Pallas kernels: 1.89 us -> 0.81 us  [per_device(): pl.pallas_call(hand_out, out_shape=(jax.ShapeDtypeStruct((SLOTS, D), BF16...]
where the time goes in v3:
time: 74 us; the launch traced here: 73.9 us
  Pallas kernels  73.2 us (99%)
    pallas_call x1, Pallas kernels, per_device(): pl.pallas_call(kernel, out_shape=(pltpu.VMEM((SLOTS, D), BF16), pltpu.VME...  72.4 us

profile of v3, /device:TPU:1, one launch (start us, length us, event | category | flops | bytes accessed | tf_op | source)
XLA Modules:
  0.0 73.9 jit_solution(13038563805968899757)
XLA Ops:
  0.6 72.4 %shard_map.113 = (bf16[16,7168]{1,0:T(8,128)(2,1)S(1)}, bf16[288,512]{1,0:T(8,128)(2,1)S(1)}) custom-call(s32[16]{0:T(128)} %len_ref.1, s32[4,16]{1,0:T(4,128)} %bitcast.11, bf16[16,64,576]{2,1,0:T(8,128)(2,1)} %q_hbm.1, bf16[16,32,576]{2,1,0:T(8,128)(2,1)} %pool_hbm.1, bf16[16,7168]{1,0:T(8,128)(2,1)} %res_hbm.1, bf16[56,128]{1,0:T(8,128)(2,1)} %bitcast.10, ...), custom_call_target="tpu_custom_call" | custom-call | flops 7000000000 | bytes 15000000 | tf_op jit(solution)/shard_map/pallas_call | solution.py:402
  73.0 0.8 %shard_map.114 = (bf16[16,7168]{1,0:T(8,128)(2,1)}, bf16[288,512]{1,0:T(8,128)(2,1)}) custom-call(bf16[16,7168]{1,0:T(8,128)(2,1)S(1)} %get-tuple-element.6.mixed_in, bf16[288,512]{1,0:T(8,128)(2,1)S(1)} %get-tuple-element.7.activ_in), custom_call_target="tpu_custom_call" | custom-call | tf_op jit(solution)/shard_map/pallas_call | solution.py:452

commit v4 on v3

--- a/solution.py
+++ b/solution.py
@@ -29,14 +29,14 @@
 FULL, TOP, BOTTOM = range(3)
 
 ORDER = (
-    ("o1", "o2"),
-    ("d0", "c10", "u0", "c20", "c00", "c02", "c01", "o3"),
-    ("d1", "u1", "u2", "d2", "c30"),
-    ("c11", "c22", "l0", "c21"),
-    ("d3", "u3", "c12", "c03"),
-    ("c32", "l1", "c31"),
-    ("l2", "c13", "l3"),
-    ("c23", "c33"),
+    "o2a", "c00b", "u0a", "c00a", "o1a", "d0a", "o2b", "o1b",
+    "c10a", "d0b", "c20a", "c20b", "c01a", "o3a", "d2a", "c02a",
+    "c01b", "u0b", "u2a", "c10b", "d1a", "c30a", "l0a", "c21a",
+    "c02b", "o3b", "u2b", "d2b", "c22a", "c11a", "c03a", "c22b",
+    "u1a", "c21b", "u3a", "c30b", "d3a", "u1b", "c12a", "l2a",
+    "c32a", "d1b", "c31a", "l0b", "u3b", "c23a", "d3b", "c12b",
+    "l1a", "l2b", "c03b", "l3a", "c11b", "c32b", "l1b", "c13a",
+    "c33a", "l3b", "c13b", "c23b", "c31b", "c33b",
 )
 
 score_scale = 192.0 ** (-0.5)
@@ -65,6 +65,21 @@
     up_a, down_a = rank_at((a + 1) % 4, b), rank_at((a + 3) % 4, b)
     up_b, down_b = rank_at(a, (b + 1) % 4), rank_at(a, (b + 3) % 4)
 
+    parts = [
+        (q_hbm.at[pl.ds(0, SL)], q_v.at[pl.ds(0, SL)]),
+        (pool_hbm, pool_v),
+        (q_hbm.at[pl.ds(SL, SL)], q_v.at[pl.ds(SL, SL)]),
+        (res_hbm, res_v),
+        (uv_hbm, uv_v),
+        (ow_hbm, ow_v),
+        (gw_hbm, gw_v),
+        (uw_hbm, uw_v),
+        (gain_hbm, gain_v),
+    ]
+    loads = [pltpu.make_async_copy(src, dst, load_sem.at[n]) for n, (src, dst) in enumerate(parts)]
+    for load in loads[:2]:
+        load.start()
+
     barrier = pltpu.get_barrier_semaphore()
 
     def greet(k, carry):
@@ -72,24 +87,7 @@
         return carry
 
     lax.fori_loop(1, N, greet, 0)
-
-    loads = [
-        pltpu.make_async_copy(src, dst, load_sem.at[i])
-        for i, (src, dst) in enumerate(
-            [
-                (q_hbm, q_v),
-                (pool_hbm, pool_v),
-                (res_hbm, res_v),
-                (uv_hbm, uv_v),
-                (ow_hbm, ow_v),
-                (gw_hbm, gw_v),
-                (uw_hbm, uw_v),
-                (gain_hbm, gain_v),
-            ]
-        )
-    ]
-    for load in loads:
-        load.start()
+    loads[2].start()
 
     lane = lax.broadcasted_iota(jnp.int32, (1, TOK), 1)
     page_of = lane // PAGE
@@ -101,19 +99,6 @@
             hit = (page_of == bt_ref[m, slot]) & (offset + m * PAGE < n)
             valid = jnp.where(hit, 1.0, valid)
         mask_v[slot // 4, slot % 4 : slot % 4 + 1, :] = valid
-    acc[...] = jnp.zeros_like(acc)
-    hid[...] = jnp.zeros_like(hid)
-    ssq[...] = jnp.zeros_like(ssq)
-    row = lax.broadcasted_iota(jnp.int32, (NC * RC, NC * RC), 0)
-    col = lax.broadcasted_iota(jnp.int32, (NC * RC, NC * RC), 1)
-    home = (row % RC) // SL * SLOTS + row // RC * SL + row % SL
-    order[...] = jnp.where(home == col, 1.0, 0.0).astype(BF16)
-    for ch in range(NC):
-        slot = lax.broadcasted_iota(jnp.int32, (SLOTS, RC), 0)
-        col = lax.broadcasted_iota(jnp.int32, (SLOTS, RC), 1)
-        hit = (slot // SL == ch) & (col == me * SL + slot % SL)
-        own_rows[ch] = jnp.where(hit, 1.0, 0.0).astype(BF16)
-
     loads[0].wait()
     loads[1].wait()
 
@@ -144,6 +129,8 @@
 
     own_ctx = []
     for ch in range(NC):
+        if ch == 1:
+            loads[2].wait()
         lax.fori_loop(ch * SL // 4, (ch + 1) * SL // 4, attend, 0)
 
         def pack(r, carry, ch=ch):
@@ -171,8 +158,11 @@
         lax.fori_loop(1, N, send_ctx, 0)
         own_ctx.append(pltpu.make_async_copy(sbuf.at[ch, me], cbuf.at[ch, me], own_sem.at[ch]))
         own_ctx[ch].start()
-
-    loads[2].wait()
+        if ch == 0:
+            for load in loads[3:]:
+                load.start()
+
+    loads[3].wait()
     for r in range(N):
         rs[r, :, 0:COLS] = res_v[:, r * COLS : (r + 1) * COLS]
         rs[r, :, COLS:LANES] = jnp.zeros((SLOTS, LANES - COLS), BF16)
@@ -189,7 +179,20 @@
     own_res = pltpu.make_async_copy(rs.at[me], rr.at[me], own_sem.at[NC])
     own_res.start()
 
-    for load in loads[3:]:
+    acc[...] = jnp.zeros_like(acc)
+    hid[...] = jnp.zeros_like(hid)
+    ssq[...] = jnp.zeros_like(ssq)
+    row = lax.broadcasted_iota(jnp.int32, (NC * RC, NC * RC), 0)
+    col = lax.broadcasted_iota(jnp.int32, (NC * RC, NC * RC), 1)
+    home = (row % RC) // SL * SLOTS + row // RC * SL + row % SL
+    order[...] = jnp.where(home == col, 1.0, 0.0).astype(BF16)
+    for ch in range(NC):
+        slot = lax.broadcasted_iota(jnp.int32, (SLOTS, RC), 0)
+        col = lax.broadcasted_iota(jnp.int32, (SLOTS, RC), 1)
+        hit = (slot // SL == ch) & (col == me * SL + slot % SL)
+        own_rows[ch] = jnp.where(hit, 1.0, 0.0).astype(BF16)
+
+    for load in loads[4:]:
         load.wait()
 
     gain_w[...] = gain_v[...].astype(F32)
@@ -299,26 +302,18 @@
 
     acts = {"o": own_line, "d": line_below, "u": line_above, "l": last_line}
 
-    def stage(g, ch, work):
-        for name in work:
+    def gather(g, early, finish):
+        left = [len(ORDER) // NC] * NC
+        for n, name in enumerate(ORDER):
+            ch = "ab".index(name[-1])
             if name[0] == "c":
                 compute(g, ch, int(name[1]), int(name[2]))
             else:
                 acts[name[0]](g, ch, int(name[1]))
-
-    def gather(g, early, finish):
-        for n, work in enumerate(ORDER):
-            def body(ch, carry, work=work):
-                stage(g, ch, work)
-                return carry
-
-            if n < len(ORDER) - 1:
-                lax.fori_loop(0, NC, body, 0)
-            else:
-                for ch in range(NC):
-                    stage(g, ch, work)
-                    finish(ch)
-            if n == 0:
+            left[ch] -= 1
+            if left[ch] == 0:
+                finish(ch)
+            if n == 6:
                 early()
 
     for ch in range(NC):
@@ -430,7 +425,7 @@
             pltpu.VMEM((NC, SLOTS, RC), BF16),
             pltpu.VMEM((NC * RC, NC * RC), BF16),
             pltpu.VMEM((NC, HID, NC * RC), F32),
-            dma((8,)),
+            dma((9,)),
             dma((NC + 1,)),
             dma,
             dma,

time: 74 us -> 72.9 us (0.985)
  Pallas kernels: 73.2 us -> 72.2 us
    pallas_call x1, Pallas kernels: 72.4 us -> 71.4 us  [per_device(): pl.pallas_call(kernel, out_shape=(pltpu.VMEM((SLOTS, D), BF16), pltpu.VME...]
where the time goes in v4:
time: 72.9 us; the launch traced here: 72.8 us
  Pallas kernels  72.2 us (99%)
    pallas_call x1, Pallas kernels, per_device(): pl.pallas_call(kernel, out_shape=(pltpu.VMEM((SLOTS, D), BF16), pltpu.VME...  71.4 us

profile of v4, /device:TPU:1, one launch (start us, length us, event | category | flops | bytes accessed | tf_op | source)
XLA Modules:
  0.0 72.8 jit_solution(5613843280487831214)
XLA Ops:
  0.6 71.4 %shard_map.113 = (bf16[16,7168]{1,0:T(8,128)(2,1)S(1)}, bf16[288,512]{1,0:T(8,128)(2,1)S(1)}) custom-call(s32[16]{0:T(128)} %len_ref.1, s32[4,16]{1,0:T(4,128)} %bitcast.11, bf16[16,64,576]{2,1,0:T(8,128)(2,1)} %q_hbm.1, bf16[16,32,576]{2,1,0:T(8,128)(2,1)} %pool_hbm.1, bf16[16,7168]{1,0:T(8,128)(2,1)} %res_hbm.1, bf16[56,128]{1,0:T(8,128)(2,1)} %bitcast.10, ...), custom_call_target="tpu_custom_call" | custom-call | flops 7000000000 | bytes 15000000 | tf_op jit(solution)/shard_map/pallas_call | solution.py:397
  72.0 0.8 %shard_map.114 = (bf16[16,7168]{1,0:T(8,128)(2,1)}, bf16[288,512]{1,0:T(8,128)(2,1)}) custom-call(bf16[16,7168]{1,0:T(8,128)(2,1)S(1)} %get-tuple-element.6.mixed_in, bf16[288,512]{1,0:T(8,128)(2,1)S(1)} %get-tuple-element.7.activ_in), custom_call_target="tpu_custom_call" | custom-call | tf_op jit(solution)/shard_map/pallas_call | solution.py:447

commit v5 on v4

--- a/solution.py
+++ b/solution.py
@@ -28,15 +28,20 @@
 
 FULL, TOP, BOTTOM = range(3)
 
+FAR_FIRST = sorted(
+    ((dy, dx, dc) for dy in range(4) for dx in range(4) for dc in range(2) if dy + dx + dc > 0),
+    key=lambda d: -(min(d[0], 4 - d[0]) + min(d[1], 4 - d[1])),
+)
+
 ORDER = (
-    "o2a", "c00b", "u0a", "c00a", "o1a", "d0a", "o2b", "o1b",
-    "c10a", "d0b", "c20a", "c20b", "c01a", "o3a", "d2a", "c02a",
-    "c01b", "u0b", "u2a", "c10b", "d1a", "c30a", "l0a", "c21a",
-    "c02b", "o3b", "u2b", "d2b", "c22a", "c11a", "c03a", "c22b",
-    "u1a", "c21b", "u3a", "c30b", "d3a", "u1b", "c12a", "l2a",
-    "c32a", "d1b", "c31a", "l0b", "u3b", "c23a", "d3b", "c12b",
-    "l1a", "l2b", "c03b", "l3a", "c11b", "c32b", "l1b", "c13a",
-    "c33a", "l3b", "c13b", "c23b", "c31b", "c33b",
+    "o1a", "o2a", "o1b", "o2b", "c00b", "d0a", "c10a", "c01a",
+    "o3a", "c10b", "d1a", "c20b", "u1a", "d2a", "c00a", "u0a",
+    "u2a", "c30a", "c11a", "c20a", "c02a", "o3b", "d1b", "c12a",
+    "c22a", "u1b", "c21a", "c11b", "u3a", "u0b", "c30b", "d3a",
+    "c12b", "d0b", "d2b", "l1a", "c32a", "c02b", "l2a", "c31a",
+    "u2b", "c21b", "u3b", "l0a", "d3b", "c23a", "c13a", "c22b",
+    "l3a", "l1b", "c32b", "c31b", "l0b", "c03a", "c33a", "l2b",
+    "l3b", "c01b", "c13b", "c03b", "c23b", "c33b",
 )
 
 score_scale = 192.0 ** (-0.5)
@@ -103,8 +108,8 @@
     loads[1].wait()
 
     def dest_of(k):
-        p = (k * 11) % N
-        return ((yy + p // 8) % 4) * 8 + ((xx + (p // 2) % 4) % 4) * 2 + (core + p % 2) % 2
+        dy, dx, dc = FAR_FIRST[k]
+        return ((yy + dy) % 4) * 8 + ((xx + dx) % 4) * 2 + (core + dc) % 2
 
     def attend(first, carry):
         q = q_v[pl.ds(first * 4, 4)].reshape(4 * HEADS, WIDTH)
@@ -155,7 +160,8 @@
             ).start()
             return carry
 
-        lax.fori_loop(1, N, send_ctx, 0)
+        for k in range(N - 1):
+            send_ctx(k, 0)
         own_ctx.append(pltpu.make_async_copy(sbuf.at[ch, me], cbuf.at[ch, me], own_sem.at[ch]))
         own_ctx[ch].start()
         if ch == 0:
@@ -175,7 +181,8 @@
         ).start()
         return carry
 
-    lax.fori_loop(1, N, send_res, 0)
+    for k in range(N - 1):
+        send_res(k, 0)
     own_res = pltpu.make_async_copy(rs.at[me], rr.at[me], own_sem.at[NC])
     own_res.start()
 

time: 72.9 us -> 72.1 us (0.989)
  Pallas kernels: 72.2 us -> 71.4 us
    pallas_call x1, Pallas kernels: 71.4 us -> 70.5 us  [per_device(): pl.pallas_call(kernel, out_shape=(pltpu.VMEM((SLOTS, D), BF16), pltpu.VME...]
where the time goes in v5:
time: 72.1 us; the launch traced here: 72 us
  Pallas kernels  71.4 us (99%)
    pallas_call x1, Pallas kernels, per_device(): pl.pallas_call(kernel, out_shape=(pltpu.VMEM((SLOTS, D), BF16), pltpu.VME...  70.5 us

profile of v5, /device:TPU:1, one launch (start us, length us, event | category | flops | bytes accessed | tf_op | source)
XLA Modules:
  0.0 72.0 jit_solution(13426182027926108065)
XLA Ops:
  0.6 70.5 %shard_map.113 = (bf16[16,7168]{1,0:T(8,128)(2,1)S(1)}, bf16[288,512]{1,0:T(8,128)(2,1)S(1)}) custom-call(s32[16]{0:T(128)} %len_ref.1, s32[4,16]{1,0:T(4,128)} %bitcast.11, bf16[16,64,576]{2,1,0:T(8,128)(2,1)} %q_hbm.1, bf16[16,32,576]{2,1,0:T(8,128)(2,1)} %pool_hbm.1, bf16[16,7168]{1,0:T(8,128)(2,1)} %res_hbm.1, bf16[56,128]{1,0:T(8,128)(2,1)} %bitcast.10, ...), custom_call_target="tpu_custom_call" | custom-call | flops 7000000000 | bytes 15000000 | tf_op jit(solution)/shard_map/pallas_call | solution.py:404
  71.2 0.8 %shard_map.114 = (bf16[16,7168]{1,0:T(8,128)(2,1)}, bf16[288,512]{1,0:T(8,128)(2,1)}) custom-call(bf16[16,7168]{1,0:T(8,128)(2,1)S(1)} %get-tuple-element.6.mixed_in, bf16[288,512]{1,0:T(8,128)(2,1)S(1)} %get-tuple-element.7.activ_in), custom_call_target="tpu_custom_call" | custom-call | tf_op jit(solution)/shard_map/pallas_call | solution.py:454
